TPU v7x, 256 devices: a whole 4x4x8 slice. The times are simulated.
256 devices in a mesh: sec: 4 (over x_lo, core), dev: 64 (over x_hi, z, y).
Axes of the slice: x: 4 (x_hi: 2, x_lo: 2; x = x_hi * 2 + x_lo), y: 4, z: 8, core: 2. Of those that a mesh axis runs over, the one named last changes fastest.
Arguments:
- queries: bfloat16 [256, 128, 576], P(('sec', 'dev')), may hold values from -56 to 56
- latent_cache: bfloat16 [256, 4096, 576], P(('sec', 'dev')), may hold values from -4 to 4
- cache_lengths: int32 [256], P(('sec', 'dev')), may hold values from 512 to 4096, as said below
- stream: bfloat16 [512, 7168], P('dev'), may hold values from -6 to 6
- norm_gain: float32 [7168], replicated, may hold values from 0.1 to 1.9
- expert_ids: int32 [512, 8], P('dev'), may hold values from 0 to 15, all different within a row; in each aligned block of 8 rows (0 to 7, 8 to 15, ...) at most 5 rows name the same one
- route_weights: float32 [512, 8], P('dev'), may hold values from 0.1 to 1
- w_gate: bfloat16 [64, 7168, 512], P('dev', None, 'sec'), may hold values from -0.0625 to 0.0625
- w_up: bfloat16 [64, 7168, 512], P('dev', None, 'sec'), may hold values from -0.0625 to 0.0625
- w_down: bfloat16 [64, 512, 7168], P('dev', 'sec'), may hold values from -0.125 to 0.125
Outputs:
- context: bfloat16 [256, 128, 512], P(('sec', 'dev'))
- mixed: bfloat16 [512, 7168], P('dev')
Inputs may be any that keep to these rules, and one draw needn't show every extreme that they name: `expert_ids`: each row names 8 distinct experts; within the 8 rows of one group no expert is named more than 5 times, a bound that some block reaches. `cache_lengths`: the longest sequence holds 4096 positions.
All inputs are finite; a program needn't handle non-finite values.
Results may differ from a plain program's by a relative error of at most 0.015.
Values may be sent and summed in bfloat16 or wider, within the bound.
No kernel may reach another device: no remote copies, remote signals or barrier semaphores. Data moves between devices by JAX's collectives and lax.ppermute only.
A program may use at most 128 MiB of HBM per device.

v0:
```python
import jax
import jax.numpy as jnp
from jax import lax
from jax.sharding import PartitionSpec as P

MOE_HIDDEN = 2048
LATENT = 512
HID_DEV = 128
score_scale = 192.0 ** (-0.5)


def slot_table(choices, count, capacity):
    experts = jnp.arange(count, dtype=jnp.int32)
    hit_count = jnp.sum((choices[..., None] == experts).astype(jnp.float32), axis=2)
    before = jnp.cumsum(hit_count, axis=1) - hit_count
    slot_ids = jnp.arange(capacity).astype(jnp.float32)
    picked = hit_count[..., None] * (before[..., None] == slot_ids).astype(jnp.float32)
    return (jnp.transpose(picked, (0, 2, 3, 1)), hit_count)


def local(
    queries,
    latent_cache,
    cache_lengths,
    stream,
    norm_gain,
    expert_ids,
    route_weights,
    w_gate,
    w_up,
    w_down,
):
    scores = (
        jnp.einsum("shk,slk->shl", queries, latent_cache, preferred_element_type=jnp.float32)
        * score_scale
    )
    visible = (
        jnp.arange(latent_cache.shape[1], dtype=jnp.int32)[None, None, :]
        < cache_lengths[:, None, None]
    )
    scores = jnp.where(visible, scores, jnp.float32(-1e30))
    peak = jnp.max(scores, axis=2, keepdims=True)
    powered = jnp.exp(scores - peak)
    probs = (powered / jnp.sum(powered, axis=2, keepdims=True)).astype(jnp.bfloat16)
    context = jnp.einsum(
        "shl,slk->shk", probs, latent_cache[:, :, :LATENT], preferred_element_type=jnp.float32
    ).astype(jnp.bfloat16)
    dev_count = lax.axis_size("dev")
    sec_count = lax.axis_size("sec")
    group_size = MOE_HIDDEN // (HID_DEV * sec_count)
    expert_count = dev_count // group_size
    row_count = stream.shape[0]
    top_count = expert_ids.shape[1]
    capacity = max(2, row_count * top_count * 5 // (4 * expert_count))
    width = stream.shape[1]
    stream_f = stream.astype(jnp.float32)
    scale_rows = lax.rsqrt(jnp.mean(stream_f * stream_f, axis=1, keepdims=True) + 1e-06)
    normed = (stream_f * scale_rows * norm_gain).astype(jnp.bfloat16)
    own_table, hit_count = slot_table(expert_ids[None], expert_count, capacity)
    own_table = own_table[0]
    all_rows, all_ids = (
        lax.all_gather(normed, "dev", axis=0, tiled=True),
        lax.all_gather(expert_ids, "dev", axis=0, tiled=True),
    )
    own_expert = lax.axis_index("dev") // group_size
    grouped_ids = all_ids.reshape(dev_count, row_count, top_count)
    named = jnp.sum((grouped_ids == own_expert).astype(jnp.float32), axis=2)
    before = jnp.cumsum(named, axis=1) - named
    slot_ids = jnp.arange(capacity).astype(jnp.float32)
    picked = named[:, None, :] * (before[:, None, :] == slot_ids[None, :, None]).astype(jnp.float32)
    received = jnp.einsum(
        "gjr,grd->gjd",
        picked.astype(jnp.bfloat16),
        all_rows.reshape(dev_count, row_count, width),
        preferred_element_type=jnp.float32,
    ).astype(jnp.bfloat16)
    slot_flat = received.reshape(dev_count * capacity, width)
    gate_proj = jnp.dot(slot_flat, w_gate[0], preferred_element_type=jnp.float32)
    up_proj = jnp.dot(slot_flat, w_up[0], preferred_element_type=jnp.float32)
    hidden = (jax.nn.silu(gate_proj) * up_proj).astype(jnp.bfloat16)
    partial_value = jnp.dot(hidden, w_down[0], preferred_element_type=jnp.float32).astype(
        jnp.bfloat16
    )
    experts = jnp.arange(expert_count, dtype=jnp.int32)
    weight_table = jnp.sum(
        route_weights[..., None] * (expert_ids[..., None] == experts).astype(jnp.float32), axis=1
    )
    weighted = own_table * jnp.transpose(weight_table)[:, None, :]
    returned = lax.all_to_all(
        partial_value.reshape(dev_count, capacity, width),
        "dev",
        split_axis=0,
        concat_axis=0,
        tiled=True,
    )
    block_sums = jnp.sum(
        returned.reshape(expert_count, group_size, capacity, width), axis=1, dtype=jnp.float32
    )
    section_part = jnp.einsum("ejr,ejd->rd", weighted, block_sums, precision=lax.Precision.HIGHEST)
    section_total = lax.psum(section_part.astype(jnp.bfloat16), "sec").astype(jnp.float32)
    mixed = (stream_f + section_total).astype(jnp.bfloat16)
    return (context, mixed)


def solution(mesh):
    return jax.shard_map(
        local,
        mesh=mesh,
        in_specs=(
            P(("sec", "dev"), None, None),
            P(("sec", "dev"), None, None),
            P(("sec", "dev")),
            P("dev", None),
            P(),
            P("dev", None),
            P("dev", None),
            P("dev", None, "sec"),
            P("dev", None, "sec"),
            P("dev", "sec", None),
        ),
        out_specs=(P(("sec", "dev"), None, None), P("dev", None)),
        check_vma=False,
    )
```

profile of v0, /device:TPU:1, one launch (start us, length us, event | category | flops | bytes accessed | tf_op | source)
XLA Modules:
  0.0 435.7 jit_solution(7749568602587736564)
XLA Ops:
  7.2 0.0 copy-start
  7.2 0.0 all-gather.2.cloned.1.call-start
  7.2 1.2 fusion.30
  8.4 1.6 fusion.32
  10.1 0.0 all-gather.2.cloned.1.call-update
  10.1 160.0 %all_gather.6 = s32[512,8]{1,0:T(8,128)S(1)} all-gather(s32[8,8]{1,0:T(8,128)} %param.15), channel_id=1, replica_groups=mesh['sec'=4,'dev'=64] {'dev'}, dimensions={0}, use_global_device_ids=true | all-gather | bytes 16640 | tf_op jit(solution)/shard_map/all_gather | solution.py:63
  170.1 0.1 convert_reduce_fusion.1
  170.3 0.1 reduce_window_sum.25
  170.4 0.2 reduce_window_sum.26
  170.6 0.0 all-gather.2.cloned.1.call-done
  170.6 8.2 %convolution_convert_fusion = bf16[64,5,7168]{2,1,0:T(8,128)(2,1)} fusion(bf16[512,7168]{1,0:T(8,128)(2,1)} %all-gather.2.cloned.1.call-done, f32[64,8]{1,0:T(8,128)S(1)} %reduce_window_sum.25, f32[64,8]{1,0:T(8,128)S(1)} %sub.33, f32[5]{0:T(128)S(1)} %iota_convert_fusion), kind=kOutput, calls=%fused_computation.1 | convolution fusion | flops 38999040 | bytes 11931668 | tf_op jit(solution)/shard_map/gjr,grd->gjd/dot_general | solution.py:71
  178.7 8.2 %reshape.143 = bf16[320,7168]{1,0:T(8,128)(2,1)} reshape(bf16[64,5,7168]{2,1,0:T(8,128)(2,1)} %convolution_convert_fusion) | data formatting | bytes 9175040 | tf_op jit(solution)/shard_map/reshape | solution.py:77
  187.0 4.2 fusion.12
  191.2 0.0 copy-done
  191.2 9.9 %convolution_convert_fusion.1 = bf16[320,7168]{1,0:T(8,128)(2,1)} fusion(bf16[1,128,7168]{2,1,0:T(8,128)(2,1)S(1)} %copy-done, bf16[320,7168]{1,0:T(8,128)(2,1)} %reshape.143, bf16[1,7168,128]{2,1,0:T(8,128)(2,1)} %param.18, f32[320,128]{1,0:T(8,128)S(1)} %fusion.12), kind=kOutput, calls=%fused_computation.2 | convolution fusion | flops 1176944640 | bytes 13008896 | tf_op jit(solution)/shard_map/dot_general | solution.py:81
  201.1 8.0 %reshape.144 = bf16[64,5,7168]{2,1,0:T(8,128)(2,1)} reshape(bf16[320,7168]{1,0:T(8,128)(2,1)} %convolution_convert_fusion.1) | data formatting | bytes 9175040 | tf_op jit(solution)/shard_map/reshape | solution.py:90
  209.1 0.0 copy-start.4
  209.1 0.0 copy-start.5
  209.1 0.0 copy-start.3
  209.1 5.9 %all-to-all-start = ((bf16[64,5,7168]{2,1,0:T(8,128)(2,1)}), bf16[64,5,7168]{2,1,0:T(8,128)(2,1)}, u32[]{:S(2)}, u32[]{:S(2)}) async-start(bf16[64,5,7168]{2,1,0:T(8,128)(2,1)} %reshape.144), calls=%async_computation | async-start | bytes 14680064 | tf_op jit(solution)/shard_map/all_to_all | solution.py:89
  215.0 0.2 all-reduce.2.cloned.1.call-start
  215.2 0.0 copy-done.4
  215.2 0.1 convert_reduce_fusion.2
  216.0 0.0 copy-done.5
  216.0 0.1 select_reduce_fusion
  216.1 0.0 copy-done.3
  216.1 3.5 fusion.55
  219.6 0.0 copy-start.1
  219.6 1.3 copy-done.1
  220.9 0.4 fusion.8
  221.3 126.4 %all-to-all-done = bf16[64,5,7168]{2,1,0:T(8,128)(2,1)} async-done(((bf16[64,5,7168]{2,1,0:T(8,128)(2,1)}), bf16[64,5,7168]{2,1,0:T(8,128)(2,1)}, u32[]{:S(2)}, u32[]{:S(2)}) %all-to-all-start) | async-done | bytes 4587552 | tf_op jit(solution)/shard_map/all_to_all | solution.py:89
  347.7 5.4 %convert_reduce_fusion = f32[16,5,7168]{2,1,0:T(8,128)S(1)} fusion(bf16[64,5,7168]{2,1,0:T(8,128)(2,1)} %all-to-all-done), kind=kLoop, calls=%fused_computation | loop fusion | flops 4014080 | bytes 6881280 | tf_op jit(solution)/shard_map/reduce_sum | solution.py:96
  353.1 4.2 fusion
  357.3 0.0 all-reduce.2.cloned.1.call-update
  357.4 0.0 copy-start.2
  357.4 5.1 %fusion.20 = bf16[1,128,512]{2,1,0:T(8,128)(2,1)} fusion(bf16[1,4096,576]{1,2,0:T(8,128)(2,1)} %param.11, f32[128,4096]{1,0:T(8,128)} %copy-done.1, f32[128]{0:T(128)S(1)} %fusion.8, f32[128]{0:T(128)S(1)} %get-tuple-element.2), kind=kOutput, calls=%fused_computation.23 | convolution fusion | flops 538509312 | bytes 6423552 | tf_op jit(solution)/shard_map/shl,slk->shk/dot_general | solution.py:45
  362.4 64.9 %all-reduce.2.cloned.1.call-done = bf16[8,7168]{1,0:T(8,128)(2,1)} async-done(((bf16[8,7168]{1,0:T(8,128)(2,1)}), bf16[8,7168]{1,0:T(8,128)(2,1)}) %all-reduce.2.cloned.1.call-update) | async-done | bytes 114704 | tf_op jit(solution)/shard_map/psum | solution.py:100
  427.3 0.0 copy-done.2
  427.3 1.6 fusion.33
  (6 shorter events, 0.1 us)
Async XLA Ops:
  7.2 184.0 %copy-start = (bf16[1,128,7168]{2,1,0:T(8,128)(2,1)S(1)}, bf16[1,128,7168]{2,1,0:T(8,128)(2,1)}, u32[]{:S(2)}) copy-start(bf16[1,128,7168]{2,1,0:T(8,128)(2,1)} %param.19) | copy-start | bytes 5505028
  7.2 163.4 %all-gather.2.cloned.1.call-start = ((), (), s32[]{:S(2)}) async-start(), calls=%async_computation.1 | async-start | bytes 7454720 | tf_op jit(solution)/shard_map/all_gather | solution.py:62
  209.1 6.1 %copy-start.4 = (s32[8,8]{1,0:T(8,128)S(1)}, s32[8,8]{1,0:T(8,128)}, u32[]{:S(2)}) copy-start(s32[8,8]{1,0:T(8,128)} %param.15) | copy-start | bytes 772
  209.1 6.9 %copy-start.5 = (f32[8,8]{1,0:T(8,128)S(1)}, f32[8,8]{1,0:T(8,128)}, u32[]{:S(2)}) copy-start(f32[8,8]{1,0:T(8,128)} %param.16) | copy-start | bytes 772
  209.1 7.0 %copy-start.3 = (bf16[1,128,576]{1,2,0:T(8,128)(2,1)S(1)}, bf16[1,128,576]{1,2,0:T(8,128)(2,1)}, u32[]{:S(2)}) copy-start(bf16[1,128,576]{1,2,0:T(8,128)(2,1)} %param.10) | copy-start | bytes 442372
  209.1 138.6 %all-to-all-start = ((bf16[64,5,7168]{2,1,0:T(8,128)(2,1)}), bf16[64,5,7168]{2,1,0:T(8,128)(2,1)}, u32[]{:S(2)}, u32[]{:S(2)}) async-start(bf16[64,5,7168]{2,1,0:T(8,128)(2,1)} %reshape.144), calls=%async_computation | async-start | bytes 14680064 | tf_op jit(solution)/shard_map/all_to_all | solution.py:89
  215.0 212.3 %all-reduce.2.cloned.1.call-start = ((), (), s32[]{:S(2)}) async-start(), calls=%async_computation.2 | async-start | bytes 229376 | tf_op jit(solution)/shard_map/psum | solution.py:100
  219.6 1.3 copy-start.1
  357.4 69.9 %copy-start.2 = (bf16[8,7168]{1,0:T(8,128)(2,1)S(1)}, bf16[8,7168]{1,0:T(8,128)(2,1)}, u32[]{:S(2)}) copy-start(bf16[8,7168]{1,0:T(8,128)(2,1)} %param.13) | copy-start | bytes 344068
Sparse Core Ops, SparseCore 0:
  12.2 145.7 all-gather.1
  357.5 69.7 all-reduce.1
where the time goes:
time: 436 us
  waiting for transfers between devices  191 us (44%)
  blocking collectives  160 us (37%)
  matrix products  35 us (8%)
  local copies, waits for them, and re-layouts  17.6 us (4%)
  between operations  14.8 us (3%)
  other arithmetic  10.8 us (2%)
  starting transfers between devices  6.12 us (1%)
    all_gather x1, blocking collectives, local(): lax.all_gather(expert_ids, 'dev', axis=0, tiled=True)  160 us
    all_to_all x1, waiting for transfers between devices, local(): lax.all_to_all(partial_value.reshape(dev_count, capacity, width), 'dev',...  126 us
    psum x1, waiting for transfers between devices, local(): lax.psum(section_part.astype(jnp.bfloat16), 'sec').astype(jnp.float32)  64.9 us
    dot_general x1, matrix products, local(): jnp.dot(hidden, w_down[0], preferred_element_type=jnp.float32)  9.9 us
  transfers between devices with their start and end apart: 3, of which 2 were waited for; matrix products, arithmetic and copies ran while one was open for 2% of the time, Pallas kernels for 0%

commit v1 on v0

--- a/solution.py
+++ b/solution.py
@@ -97,7 +97,9 @@
         returned.reshape(expert_count, group_size, capacity, width), axis=1, dtype=jnp.float32
     )
     section_part = jnp.einsum("ejr,ejd->rd", weighted, block_sums, precision=lax.Precision.HIGHEST)
-    section_total = lax.psum(section_part.astype(jnp.bfloat16), "sec").astype(jnp.float32)
+    section_total = jnp.sum(
+        lax.all_gather(section_part.astype(jnp.bfloat16), "sec"), axis=0
+    ).astype(jnp.float32)
     mixed = (stream_f + section_total).astype(jnp.bfloat16)
     return (context, mixed)
 

time: 436 us -> 403 us (0.924)
  waiting for transfers between devices: 191 us -> 123 us
  blocking collectives: 160 us -> 197 us
    psum x1 -> x0, waiting for transfers between devices: 64.9 us -> none  [local(): lax.psum(section_part.astype(jnp.bfloat16), 'sec').astype(jnp.float32)]
    all_gather x0 -> x1, blocking collectives: none -> 37.4 us  [local(): lax.all_gather(section_part.astype(jnp.bfloat16), 'sec')]
  transfers between devices with their start and end apart: 3 -> 2, of which waited for: 2 -> 1; matrix products, arithmetic and copies ran while one was open for 2% -> 2% of each run, Pallas kernels for 0% -> 0%
where the time goes in v1:
time: 403 us; the launch traced here: 402 us
  blocking collectives  197 us (49%)
  waiting for transfers between devices  123 us (31%)
  matrix products  33.7 us (8%)
  local copies, waits for them, and re-layouts  16.3 us (4%)
  between operations  14.8 us (4%)
  other arithmetic  9.93 us (2%)
  starting transfers between devices  6.08 us (2%)
    all_gather x1, blocking collectives, local(): lax.all_gather(expert_ids, 'dev', axis=0, tiled=True)  160 us
    all_to_all x1, waiting for transfers between devices, local(): lax.all_to_all(partial_value.reshape(dev_count, capacity, width), 'dev',...  123 us
    all_gather x1, blocking collectives, local(): lax.all_gather(section_part.astype(jnp.bfloat16), 'sec')  37.4 us
    dot_general x1, matrix products, local(): jnp.dot(hidden, w_down[0], preferred_element_type=jnp.float32)  9.9 us
    reshape x1, local copies, waits for them, and re-layouts, local(): slot_flat = received.reshape(dev_count * capacity, width)  8.22 us
    dot_general x1, matrix products, local(): jnp.einsum('gjr,grd->gjd', picked.astype(jnp.bfloat16), all_rows.reshape(...  8.17 us
  transfers between devices with their start and end apart: 2, of which 1 were waited for; matrix products, arithmetic and copies ran while one was open for 2% of the time, Pallas kernels for 0%

profile of v1, /device:TPU:1, one launch (start us, length us, event | category | flops | bytes accessed | tf_op | source)
XLA Modules:
  0.0 401.7 jit_solution(2059073587830426192)
XLA Ops:
  7.2 0.0 copy-start
  7.2 0.0 all-gather.3.cloned.1.call-start
  7.2 1.2 fusion.30
  8.4 1.6 fusion.32
  10.1 0.0 all-gather.3.cloned.1.call-update
  10.1 160.0 %all_gather.12 = s32[512,8]{1,0:T(8,128)S(1)} all-gather(s32[8,8]{1,0:T(8,128)} %param.15), channel_id=1, replica_groups=mesh['sec'=4,'dev'=64] {'dev'}, dimensions={0}, use_global_device_ids=true | all-gather | bytes 16640 | tf_op jit(solution)/shard_map/all_gather | solution.py:63
  170.1 0.1 convert_reduce_fusion.1
  170.3 0.1 reduce_window_sum.25
  170.4 0.2 reduce_window_sum.26
  170.6 0.0 all-gather.3.cloned.1.call-done
  170.6 8.2 %convolution_convert_fusion = bf16[64,5,7168]{2,1,0:T(8,128)(2,1)} fusion(bf16[512,7168]{1,0:T(8,128)(2,1)} %all-gather.3.cloned.1.call-done, f32[64,8]{1,0:T(8,128)S(1)} %reduce_window_sum.25, f32[64,8]{1,0:T(8,128)S(1)} %sub.33, f32[5]{0:T(128)S(1)} %iota_convert_fusion), kind=kOutput, calls=%fused_computation.1 | convolution fusion | flops 38999040 | bytes 11931668 | tf_op jit(solution)/shard_map/gjr,grd->gjd/dot_general | solution.py:71
  178.7 8.2 %reshape.143 = bf16[320,7168]{1,0:T(8,128)(2,1)} reshape(bf16[64,5,7168]{2,1,0:T(8,128)(2,1)} %convolution_convert_fusion) | data formatting | bytes 9175040 | tf_op jit(solution)/shard_map/reshape | solution.py:77
  187.0 4.2 %fusion.12 = f32[320,128]{1,0:T(8,128)S(1)} fusion(bf16[320,7168]{1,0:T(8,128)(2,1)} %reshape.143, bf16[1,7168,128]{2,1,0:T(8,128)(2,1)} %param.17), kind=kOutput, calls=%fused_computation.19 | convolution fusion | flops 587202560 | bytes 6586368 | tf_op jit(solution)/shard_map/dot_general | solution.py:78
  191.2 0.0 copy-done
  191.2 9.9 %convolution_convert_fusion.1 = bf16[320,7168]{1,0:T(8,128)(2,1)} fusion(bf16[1,128,7168]{2,1,0:T(8,128)(2,1)S(1)} %copy-done, bf16[320,7168]{1,0:T(8,128)(2,1)} %reshape.143, bf16[1,7168,128]{2,1,0:T(8,128)(2,1)} %param.18, f32[320,128]{1,0:T(8,128)S(1)} %fusion.12), kind=kOutput, calls=%fused_computation.2 | convolution fusion | flops 1176944640 | bytes 13008896 | tf_op jit(solution)/shard_map/dot_general | solution.py:81
  201.1 8.0 %reshape.144 = bf16[64,5,7168]{2,1,0:T(8,128)(2,1)} reshape(bf16[320,7168]{1,0:T(8,128)(2,1)} %convolution_convert_fusion.1) | data formatting | bytes 9175040 | tf_op jit(solution)/shard_map/reshape | solution.py:90
  209.1 0.0 copy-start.3
  209.1 0.0 copy-start.4
  209.1 0.0 copy-start.2
  209.1 6.0 %all-to-all-start = ((bf16[64,5,7168]{2,1,0:T(8,128)(2,1)}), bf16[64,5,7168]{2,1,0:T(8,128)(2,1)}, u32[]{:S(2)}, u32[]{:S(2)}) async-start(bf16[64,5,7168]{2,1,0:T(8,128)(2,1)} %reshape.144), calls=%async_computation | async-start | bytes 14680064 | tf_op jit(solution)/shard_map/all_to_all | solution.py:89
  215.1 0.0 copy-done.3
  215.2 0.1 convert_reduce_fusion.2
  215.9 0.0 copy-done.4
  216.0 0.1 select_reduce_fusion
  216.1 0.0 copy-done.2
  216.1 3.5 fusion.55
  219.5 0.4 fusion.8
  220.0 4.4 %fusion.20 = bf16[1,128,512]{2,1,0:T(8,128)(2,1)} fusion(bf16[1,4096,576]{1,2,0:T(8,128)(2,1)} %param.11, f32[128,4096]{1,0:T(8,128)S(1)} %get-tuple-element.3, f32[128]{0:T(128)S(1)} %fusion.8, f32[128]{0:T(128)S(1)} %get-tuple-element.2), kind=kOutput, calls=%fused_computation.23 | convolution fusion | flops 538509312 | bytes 6423552 | tf_op jit(solution)/shard_map/shl,slk->shk/dot_general | solution.py:45
  224.4 0.0 copy-start.1
  224.4 123.4 %all-to-all-done = bf16[64,5,7168]{2,1,0:T(8,128)(2,1)} async-done(((bf16[64,5,7168]{2,1,0:T(8,128)(2,1)}), bf16[64,5,7168]{2,1,0:T(8,128)(2,1)}, u32[]{:S(2)}, u32[]{:S(2)}) %all-to-all-start) | async-done | bytes 4587552 | tf_op jit(solution)/shard_map/all_to_all | solution.py:89
  347.7 5.4 %convert_reduce_fusion = f32[16,5,7168]{2,1,0:T(8,128)S(1)} fusion(bf16[64,5,7168]{2,1,0:T(8,128)(2,1)} %all-to-all-done), kind=kLoop, calls=%fused_computation | loop fusion | flops 4014080 | bytes 6881280 | tf_op jit(solution)/shard_map/reduce_sum | solution.py:96
  353.1 3.6 fusion
  356.7 37.4 %all-gather = bf16[32,7168]{1,0:T(8,128)(2,1)S(1)} all-gather(bf16[8,7168]{1,0:T(8,128)(2,1)S(1)} %fusion), channel_id=2, replica_groups=mesh['sec'=4,'dev'=64] {'sec'}, dimensions={0}, use_global_device_ids=true | all-gather | bytes 573440 | tf_op jit(solution)/shard_map/all_gather | solution.py:101
  394.1 0.1 bitcast_reduce_fusion
  394.2 0.0 copy-done.1
  394.2 0.7 fusion.33
  (6 shorter events, 0.1 us)
Async XLA Ops:
  7.2 184.0 %copy-start = (bf16[1,128,7168]{2,1,0:T(8,128)(2,1)S(1)}, bf16[1,128,7168]{2,1,0:T(8,128)(2,1)}, u32[]{:S(2)}) copy-start(bf16[1,128,7168]{2,1,0:T(8,128)(2,1)} %param.19) | copy-start | bytes 5505028
  7.2 163.4 %all-gather.3.cloned.1.call-start = ((), (), s32[]{:S(2)}) async-start(), calls=%async_computation.1 | async-start | bytes 7454720 | tf_op jit(solution)/shard_map/all_gather | solution.py:62
  209.1 6.1 %copy-start.3 = (s32[8,8]{1,0:T(8,128)S(1)}, s32[8,8]{1,0:T(8,128)}, u32[]{:S(2)}) copy-start(s32[8,8]{1,0:T(8,128)} %param.15) | copy-start | bytes 772
  209.1 6.9 %copy-start.4 = (f32[8,8]{1,0:T(8,128)S(1)}, f32[8,8]{1,0:T(8,128)}, u32[]{:S(2)}) copy-start(f32[8,8]{1,0:T(8,128)} %param.16) | copy-start | bytes 772
  209.1 7.0 %copy-start.2 = (bf16[1,128,576]{1,2,0:T(8,128)(2,1)S(1)}, bf16[1,128,576]{1,2,0:T(8,128)(2,1)}, u32[]{:S(2)}) copy-start(bf16[1,128,576]{1,2,0:T(8,128)(2,1)} %param.10) | copy-start | bytes 442372
  209.1 138.6 %all-to-all-start = ((bf16[64,5,7168]{2,1,0:T(8,128)(2,1)}), bf16[64,5,7168]{2,1,0:T(8,128)(2,1)}, u32[]{:S(2)}, u32[]{:S(2)}) async-start(bf16[64,5,7168]{2,1,0:T(8,128)(2,1)} %reshape.144), calls=%async_computation | async-start | bytes 14680064 | tf_op jit(solution)/shard_map/all_to_all | solution.py:89
  224.4 169.8 %copy-start.1 = (bf16[8,7168]{1,0:T(8,128)(2,1)S(1)}, bf16[8,7168]{1,0:T(8,128)(2,1)}, u32[]{:S(2)}) copy-start(bf16[8,7168]{1,0:T(8,128)(2,1)} %param.13) | copy-start | bytes 344068
Sparse Core Ops, SparseCore 0:
  12.2 145.7 all-gather.2
